TPU v7x, 512 devices: a whole 4x4x16 slice. The times are simulated.
512 devices in a mesh: row: 32 (over z_lo, y), col: 16 (over z_hi, x, core).
Axes of the slice: x: 4, y: 4, z: 16 (z_hi: 2, z_lo: 8; z = z_hi * 8 + z_lo), core: 2. Of those that a mesh axis runs over, the one named last changes fastest.
Arguments:
- entries: int32 [128, 64, 128, 128], P('row', 'col'), may hold values from -2 to 2
- tile_cols: int32 [128, 64], P('row', 'col'), may hold values from 0 to 31
- block_now: int32 [32, 65536], P(None, ('col', 'row')), may hold values from 0 to 65520
- block_prev: int32 [32, 65536], P(None, ('col', 'row')), may hold values from 0 to 65520
- block_prev2: int32 [32, 65536], P(None, ('col', 'row')), may hold values from 0 to 65520
- gram_prev: int32 [32, 32], replicated, may hold values from 0 to 65520
- square_prev: int32 [32, 32], replicated, may hold values from 0 to 65520
- inverse_prev: int32 [32, 32], replicated, may hold values from 0 to 65520
- inverse_prev2: int32 [32, 32], replicated, may hold values from 0 to 65520
Outputs:
- next_block: float32 [32, 65536], P(None, ('col', 'row'))
- later_block: float32 [32, 65536], P(None, ('col', 'row'))
Inputs may be any that keep to these rules, and one draw needn't show every extreme that they name: `tile_cols`: stored tiles that name the same tile column in one tile row add. `block_prev`: residues. `block_prev2`: residues. `gram_prev`: residues. `square_prev`: residues. `inverse_prev`: residues. `inverse_prev2`: residues.
All inputs are finite; a program needn't handle non-finite values.
Results may differ from a plain program's by a relative error of at most 0.0003.
Values sent between devices are 32-bit elements; how exact they have to be, the bound alone decides.
No kernel may reach another device: no remote copies, remote signals or barrier semaphores. Data moves between devices by JAX's collectives and lax.ppermute only.
A program may use at most 64 MiB of HBM per device.

v0:
```python
import jax
import jax.numpy as jnp
from jax import lax
from jax.sharding import PartitionSpec as P

modulus = 65521.0


def residue(values):
    return jnp.mod(values, modulus)


def split_digits(values):
    top_part = jnp.floor(values / 256.0)
    return (top_part, values - top_part * 256.0)


def fold_digits(top_sum, low_sum):
    return residue(residue(residue(top_sum) * 256.0) + residue(low_sum))


def fold_three(upper_part, middle, lower_part):
    return residue(
        residue(residue(upper_part) * 15.0) + residue(residue(middle) * 256.0) + residue(lower_part)
    )


def mulmod(left_side, right_side):
    top_part, low_part = split_digits(right_side)
    return fold_digits(left_side * top_part, left_side * low_part)


def exact_dot(left_side, right_side):
    return jnp.dot(
        left_side, right_side, precision=lax.Precision.HIGHEST, preferred_element_type=jnp.float32
    )


def small_product(left_side, right_side):
    left_top, left_low = split_digits(left_side)
    right_top, right_low = split_digits(right_side)
    return fold_three(
        exact_dot(left_top, right_top),
        exact_dot(left_top, right_low) + exact_dot(left_low, right_top),
        exact_dot(left_low, right_low),
    )


def inverse_scalar(number):
    result = jnp.ones_like(number)
    square = number
    exponent = 65519
    for position in range(16):
        if exponent >> position & 1:
            result = mulmod(result, square)
        square = mulmod(square, square)
    return result


def inverse_matrix(matrix):
    matrix_order = matrix.shape[0]
    augmented = jnp.concatenate([matrix, jnp.eye(matrix_order, dtype=matrix.dtype)], axis=1)
    row_numbers = jnp.arange(matrix_order, dtype=jnp.int32)

    def eliminate(column, augmented):
        column = jnp.asarray(column).astype(jnp.int32)
        pivot_column = augmented[:, column]
        usable = (pivot_column != 0.0) & (row_numbers >= column)
        pivot_row_id = jnp.where(jnp.any(usable), jnp.argmax(usable), column)
        pivot_row = augmented[pivot_row_id]
        current_row = augmented[column]
        swapped = jnp.where(
            (row_numbers == column)[:, None],
            pivot_row[None, :],
            jnp.where((row_numbers == pivot_row_id)[:, None], current_row[None, :], augmented),
        )
        scaled = mulmod(pivot_row, inverse_scalar(pivot_row[column]))
        factors = jnp.where(row_numbers == column, 0.0, swapped[:, column])
        reduced = residue(swapped - mulmod(factors[:, None], scaled[None, :]) + modulus)
        return jnp.where((row_numbers == column)[:, None], scaled[None, :], reduced)

    augmented = lax.fori_loop(0, matrix_order, eliminate, augmented)
    return augmented[:, matrix_order:]


def coefficients(
    gram_now, square_now, inverse_now, inverse_prev, inverse_prev2, gram_old, square_old
):
    identity = jnp.eye(gram_now.shape[0], dtype=gram_now.dtype)
    first = residue(identity - small_product(residue(square_now + gram_now), inverse_now) + modulus)
    second = residue(modulus - small_product(gram_now, inverse_prev))
    middle = residue(identity - small_product(inverse_prev, gram_old) + modulus)
    third = residue(
        modulus
        - small_product(small_product(residue(square_old + gram_old), middle), inverse_prev2)
    )
    return jnp.concatenate([first, second, third], axis=1)


def digit_stack(values):
    top_part, low_part = split_digits(values)
    return jnp.stack([top_part, low_part]).astype(jnp.bfloat16)


def combine_blocks(coeffs, stacked):
    products = jnp.einsum(
        "dab,ebn->dean",
        digit_stack(coeffs),
        digit_stack(stacked),
        preferred_element_type=jnp.float32,
    )
    return fold_three(products[0, 0], products[0, 1] + products[1, 0], products[1, 1])


def gram_local(first, second):
    column_count = first.shape[1]
    group_width = min(column_count, 128)
    groups = column_count // group_width
    first_digits = digit_stack(first).reshape(2, first.shape[0], groups, group_width)
    second_digits = digit_stack(second).reshape(2, second.shape[0], groups, group_width)
    products = jnp.einsum(
        "dagw,ecgw->gdeac", first_digits, second_digits, preferred_element_type=jnp.float32
    )
    per_group = fold_three(
        products[:, 0, 0], products[:, 0, 1] + products[:, 1, 0], products[:, 1, 1]
    )
    return residue(jnp.sum(per_group, axis=0))


def digit_pair(values):
    top_part, low_part = split_digits(values)
    return jnp.stack([top_part, low_part])


def forward_partial(block_full, tile_values, tile_cols):
    tile_rows, slot_count, tile_size = (
        tile_values.shape[0],
        tile_values.shape[1],
        tile_values.shape[2],
    )
    block_rows = block_full.shape[0]
    top_part, low_part = split_digits(block_full)
    digits = jnp.concatenate([top_part, low_part], axis=0).astype(jnp.bfloat16)
    digits = digits.reshape(2 * block_rows, -1, tile_size)
    picked = jnp.take(digits, tile_cols.reshape(-1), axis=1).reshape(
        2 * block_rows, tile_rows, slot_count, tile_size
    )
    raw_sums = jnp.einsum("brsk,rsjk->brj", picked, tile_values, preferred_element_type=jnp.float32)
    return fold_digits(raw_sums[:block_rows], raw_sums[block_rows:]).reshape(
        block_rows, tile_rows * tile_size
    )


def backward_partial(projected, tile_values, onehot):
    tile_rows, tile_size = (tile_values.shape[0], tile_values.shape[2])
    block_rows = projected.shape[0]
    top_part, low_part = split_digits(projected)
    digits = (
        jnp.concatenate([top_part, low_part], axis=0)
        .astype(jnp.bfloat16)
        .reshape(2 * block_rows, tile_rows, tile_size)
    )
    spread = jnp.einsum("brj,rsjk->brsk", digits, tile_values, preferred_element_type=jnp.float32)
    raw_sums = jnp.einsum(
        "brsk,rsc->bck",
        spread,
        onehot,
        precision=lax.Precision.HIGHEST,
        preferred_element_type=jnp.float32,
    )
    return fold_digits(raw_sums[:block_rows], raw_sums[block_rows:]).reshape(block_rows, -1)


def body(
    entries,
    tile_cols,
    block_now,
    block_prev,
    block_prev2,
    gram_prev,
    square_prev,
    inverse_prev,
    inverse_prev2,
):
    tile_values = entries.astype(jnp.bfloat16)
    tile_size = tile_values.shape[2]
    share_width = block_now.shape[1]
    col_tiles = share_width * lax.axis_size("row") // tile_size
    onehot = (
        tile_cols[:, :, None] == jnp.arange(col_tiles, dtype=jnp.int32)[None, None, :]
    ).astype(jnp.float32)
    current = block_now.astype(jnp.float32)
    earlier = block_prev.astype(jnp.float32)
    earliest = block_prev2.astype(jnp.float32)
    gram_old = gram_prev.astype(jnp.float32)
    square_old = square_prev.astype(jnp.float32)
    inverse_old = inverse_prev.astype(jnp.float32)
    inverse_older = inverse_prev2.astype(jnp.float32)
    results = []
    for iteration in range(2):
        block_full = lax.all_gather(current, "row", axis=1, tiled=True)
        projected = residue(lax.psum(forward_partial(block_full, tile_values, tile_cols), "col"))
        partial_term = backward_partial(projected, tile_values, onehot)
        applied = residue(lax.psum_scatter(partial_term, "row", scatter_dimension=1, tiled=True))
        current_own = current
        both_sums = lax.psum(
            jnp.stack(
                [
                    digit_pair(gram_local(current_own, applied)),
                    digit_pair(gram_local(applied, applied)),
                ]
            ),
            ("row", "col"),
        )
        gram_now = fold_digits(both_sums[0, 0], both_sums[0, 1])
        square_now = fold_digits(both_sums[1, 0], both_sums[1, 1])
        inverse_now = inverse_matrix(gram_now)
        coeffs = coefficients(
            gram_now, square_now, inverse_now, inverse_old, inverse_older, gram_old, square_old
        )
        stacked = jnp.concatenate([current, earlier, earliest], axis=0)
        following = residue(applied + combine_blocks(coeffs, stacked))
        results.append(following / modulus)
        earliest, earlier, current = (earlier, current, following)
        inverse_older, inverse_old = (inverse_old, inverse_now)
        gram_old, square_old = (gram_now, square_now)
    return (results[0], results[1])


def solution(mesh):
    placed = (
        P("row", "col", None, None),
        P("row", "col"),
        P(None, ("col", "row")),
        P(None, ("col", "row")),
        P(None, ("col", "row")),
        P(),
        P(),
        P(),
        P(),
    )
    return jax.shard_map(
        body,
        mesh=mesh,
        in_specs=placed,
        out_specs=(P(None, ("col", "row")), P(None, ("col", "row"))),
        check_vma=False,
    )
```

profile of v0, /device:TPU:1, one launch (start us, length us, event | category | flops | bytes accessed | tf_op | source)
XLA Modules:
  0.0 2244.6 jit_solution(948067549384732013)
XLA Ops:
  7.2 0.8 reshape.1652
  8.8 114.7 %all_gather.6 = f32[32,4096]{1,0:T(8,128)S(1)} all-gather(f32[32,128]{1,0:T(8,128)S(1)} %get-tuple-element.319), channel_id=1, replica_groups=mesh['row'=32,'col'=16] {'row'}, dimensions={1}, use_global_device_ids=true | all-gather | bytes 540672 | tf_op jit(solution)/shard_map/all_gather | solution.py:201
  124.9 0.8 copy_bitcast_fusion.7
  129.3 247.2 %all-reduce.3.cloned.1.call-done = f32[32,512]{1,0:T(8,128)} async-done(((f32[32,512]{1,0:T(8,128)}), f32[32,512]{1,0:T(8,128)}) %all-reduce.3.cloned.1.call-update) | async-done | bytes 65552 | tf_op jit(solution)/shard_map/psum | solution.py:202
  376.5 0.9 fusion.102
  378.1 1.1 convolution_bitcast_fusion.1
  379.2 1.1 add_select_fusion.22
  380.3 1.1 copy.355
  383.5 212.7 %reduce-scatter.3.cloned.1.call-done = f32[32,128]{1,0:T(8,128)} async-done(((f32[32,4096]{1,0:T(8,128)}), f32[32,128]{1,0:T(8,128)}) %reduce-scatter.3.cloned.1.call-update) | async-done | bytes 16400 | tf_op jit(solution)/shard_map/reduce_scatter | solution.py:204
  596.2 0.7 fusion.339
  597.5 125.4 %psum.29 = f32[2,2,32,32]{2,3,1,0:T(8,128)S(1)} all-reduce(f32[2,2,32,32]{2,3,1,0:T(8,128)S(1)} %pad_maximum_fusion.2), channel_id=1, replica_groups=mesh['row'=32,'col'=16] {'row','col'}, use_global_device_ids=true, to_apply=%region_2.4 | all-reduce | flops 4096 | bytes 32768 | tf_op jit(solution)/shard_map/psum | solution.py:206
  722.9 403.5 %while.36 = (s32[]{:T(128)}, f32[32,64]{0,1:T(8,128)S(1)}, s32[]{:T(128)}, s32[]{:T(128)}, s32[]{:T(128)}, /*index=5*/s32[]{:T(128)}, s32[]{:T(128)}, f32[]{:T(128)}, f32[]{:T(128)}, f32[]{:T(128)}, /*index=10*/f32[]{:T(128)}) while((s32[]{:T(128)}, f32[32,64]{0,1:T(8,128)S(1)}, s32[]{:T(128)}, s32[]{:T(128)}, ...), condition=%wide.region_6.8_spmd.clone.clone, body=%wide.region_3.7_spmd.clone.clone.sunk | while | flops 87498 | bytes 50118 | solution.py:82
  723.6 0.7 iota_reduce_fusion.4
  736.2 0.7 iota_reduce_fusion.4
  761.4 0.7 iota_reduce_fusion.4
  799.3 0.7 iota_reduce_fusion.4
  837.1 0.7 iota_reduce_fusion.4
  862.3 0.7 iota_reduce_fusion.4
  874.9 0.7 iota_reduce_fusion.4
  900.1 0.7 iota_reduce_fusion.4
  938.0 0.7 iota_reduce_fusion.4
  1129.8 103.1 %all_gather.7 = f32[32,4096]{1,0:T(8,128)S(1)} all-gather(f32[32,128]{1,0:T(8,128)S(1)} %get-tuple-element.280), channel_id=1, replica_groups=mesh['row'=32,'col'=16] {'row'}, dimensions={1}, use_global_device_ids=true | all-gather | bytes 540672 | tf_op jit(solution)/shard_map/all_gather | solution.py:201
  1234.2 0.8 copy_bitcast_fusion.6
  1235.6 249.9 %all-reduce.5.cloned.1.call-done = f32[32,512]{1,0:T(8,128)} async-done(((f32[32,512]{1,0:T(8,128)}), f32[32,512]{1,0:T(8,128)}) %all-reduce.5.cloned.1.call-update) | async-done | bytes 65552 | tf_op jit(solution)/shard_map/psum | solution.py:202
  1485.5 0.9 fusion.103
  1486.7 1.1 convolution_bitcast_fusion
  1487.7 1.1 add_select_fusion.18
  1488.9 1.1 copy.354
  1491.4 213.1 %reduce-scatter.5.cloned.1.call-done = f32[32,128]{1,0:T(8,128)} async-done(((f32[32,4096]{1,0:T(8,128)}), f32[32,128]{1,0:T(8,128)}) %reduce-scatter.5.cloned.1.call-update) | async-done | bytes 16400 | tf_op jit(solution)/shard_map/reduce_scatter | solution.py:204
  1704.5 0.7 fusion.343
  1705.8 125.7 %psum.31 = f32[2,2,32,32]{2,3,1,0:T(8,128)S(1)} all-reduce(f32[2,2,32,32]{2,3,1,0:T(8,128)S(1)} %pad_maximum_fusion.3), channel_id=1, replica_groups=mesh['row'=32,'col'=16] {'row','col'}, use_global_device_ids=true, to_apply=%region_9.11 | all-reduce | flops 4096 | bytes 32768 | tf_op jit(solution)/shard_map/psum | solution.py:206
  1831.6 403.5 %while.37 = (s32[]{:T(128)}, f32[32,64]{0,1:T(8,128)S(1)}, s32[]{:T(128)}, s32[]{:T(128)}, s32[]{:T(128)}, /*index=5*/s32[]{:T(128)}, s32[]{:T(128)}, f32[]{:T(128)}, f32[]{:T(128)}, f32[]{:T(128)}, /*index=10*/f32[]{:T(128)}) while((s32[]{:T(128)}, f32[32,64]{0,1:T(8,128)S(1)}, s32[]{:T(128)}, s32[]{:T(128)}, ...), condition=%wide.region_13.15_spmd.clone.clone, body=%wide.region_10.14_spmd.clone.clone.sunk | while | flops 87498 | bytes 50118 | solution.py:82
  (706 shorter events, 178.9 us)
Async XLA Ops:
  7.2 116.5 %copy-start = (s32[4,4,128,128]{3,2,1,0:T(8,128)S(1)}, s32[4,4,128,128]{3,2,1,0:T(8,128)}, u32[]{:S(2)}) copy-start(s32[4,4,128,128]{3,2,1,0:T(8,128)} %param.15) | copy-start | bytes 3145732
  7.2 369.3 %all-reduce.3.cloned.1.call-start = ((), (), s32[]{:S(2)}) async-start(), calls=%async_computation.2 | async-start | bytes 131072 | tf_op jit(solution)/shard_map/psum | solution.py:202
  125.7 0.7 copy-start.5
  125.7 0.8 copy-start.6
  125.7 470.4 %reduce-scatter.3.cloned.1.call-start = ((), (), s32[]{:S(2)}) async-start(), calls=%async_computation.3 | async-start | bytes 540672 | tf_op jit(solution)/shard_map/reduce_scatter | solution.py:204
  126.9 0.7 copy-start.7
  128.2 0.7 copy-start.8
  377.4 0.7 copy-start.4
  381.5 1104.0 %all-reduce.5.cloned.1.call-start = ((), (), s32[]{:S(2)}) async-start(), calls=%async_computation.4 | async-start | bytes 131072 | tf_op jit(solution)/shard_map/psum | solution.py:202
  382.0 0.7 copy-start.9
  382.0 0.7 copy-start.10
  382.8 0.7 copy-start.1
  1129.0 0.7 copy-start.2
  1235.0 469.5 %reduce-scatter.5.cloned.1.call-start = ((), (), s32[]{:S(2)}) async-start(), calls=%async_computation.5 | async-start | bytes 540672 | tf_op jit(solution)/shard_map/reduce_scatter | solution.py:204
  2236.6 0.7 copy-start.3
Sparse Core Ops, SparseCore 0:
  125.8 250.6 all-reduce.2
  381.6 214.5 reduce-scatter.2
  1235.1 250.3 all-reduce.4
  1490.1 214.3 reduce-scatter.4
where the time goes:
time: 2250 us; the launch traced here: 2240 us
  waiting for transfers between devices  923 us (41%)
  loops' own time  641 us (28%)
  blocking collectives  469 us (21%)
  other arithmetic  139 us (6%)
  local copies, waits for them, and re-layouts  47.5 us (2%)
    another operation x2, loops' own time, inverse_matrix(): augmented = lax.fori_loop(0, matrix_order, eliminate, augmented)  641 us
    psum x2, waiting for transfers between devices, body(): lax.psum(forward_partial(block_full, tile_values, tile_cols), 'col')  497 us
    reduce_scatter x2, waiting for transfers between devices, body(): lax.psum_scatter(partial_term, 'row', scatter_dimension=1, tiled=True)  426 us
    psum x2, blocking collectives, body(): lax.psum(jnp.stack([digit_pair(gram_local(current_own, applied)), digit_p...  251 us
    all_gather x2, blocking collectives, body(): block_full = lax.all_gather(current, 'row', axis=1, tiled=True)  218 us
    another operation x64, other arithmetic, eliminate(): pivot_row_id = jnp.where(jnp.any(usable), jnp.argmax(usable), column)  46.5 us
  transfers between devices with their start and end apart: 4, of which 4 were waited for; matrix products, arithmetic and copies ran while one was open for 0% of the time, Pallas kernels for 0%

commit v1 on v0

--- a/solution.py
+++ b/solution.py
@@ -2,6 +2,7 @@
 import jax.numpy as jnp
 from jax import lax
 from jax.sharding import PartitionSpec as P
+from jax.lax import all_gather
 
 modulus = 65521.0
 
@@ -199,7 +200,12 @@
     results = []
     for iteration in range(2):
         block_full = lax.all_gather(current, "row", axis=1, tiled=True)
-        projected = residue(lax.psum(forward_partial(block_full, tile_values, tile_cols), "col"))
+        projected = residue(
+            jnp.sum(
+                all_gather(forward_partial(block_full, tile_values, tile_cols), axis_name="col"),
+                axis=0,
+            )
+        )
         partial_term = backward_partial(projected, tile_values, onehot)
         applied = residue(lax.psum_scatter(partial_term, "row", scatter_dimension=1, tiled=True))
         current_own = current

time: 2250 us -> 1910 us (0.85)
  waiting for transfers between devices: 923 us -> 575 us
    psum x2 -> x0, waiting for transfers between devices: 497 us -> none  [body(): lax.psum(forward_partial(block_full, tile_values, tile_cols), 'col')]
    all_gather x0 -> x2, waiting for transfers between devices: none -> 168 us  [body(): all_gather(forward_partial(block_full, tile_values, tile_cols), axis_name...]
where the time goes in v1:
time: 1910 us
  loops' own time  648 us (34%)
  waiting for transfers between devices  575 us (30%)
  blocking collectives  469 us (25%)
  other arithmetic  140 us (7%)
  local copies, waits for them, and re-layouts  51.6 us (3%)
    another operation x2, loops' own time, inverse_matrix(): augmented = lax.fori_loop(0, matrix_order, eliminate, augmented)  648 us
    reduce_scatter x2, waiting for transfers between devices, body(): lax.psum_scatter(partial_term, 'row', scatter_dimension=1, tiled=True)  407 us
    psum x2, blocking collectives, body(): lax.psum(jnp.stack([digit_pair(gram_local(current_own, applied)), digit_p...  251 us
    all_gather x2, blocking collectives, body(): block_full = lax.all_gather(current, 'row', axis=1, tiled=True)  217 us
    all_gather x2, waiting for transfers between devices, body(): all_gather(forward_partial(block_full, tile_values, tile_cols), axis_name...  168 us
    another operation x64, other arithmetic, eliminate(): pivot_row_id = jnp.where(jnp.any(usable), jnp.argmax(usable), column)  44.7 us
    eq x64, other arithmetic, eliminate(): return jnp.where((row_numbers == column)[:, None], scaled[None, :], reduced)  43.8 us
    dynamic_slice x64, local copies, waits for them, and re-layouts, eliminate(): scaled = mulmod(pivot_row, inverse_scalar(pivot_row[column]))  40.2 us
  transfers between devices with their start and end apart: 4, of which 4 were waited for; matrix products, arithmetic and copies ran while one was open for 0% of the time, Pallas kernels for 0%

profile of v1, /device:TPU:1, one launch (start us, length us, event | category | flops | bytes accessed | tf_op | source)
XLA Modules:
  0.0 1908.0 jit_solution(9665272047162300574)
XLA Ops:
  7.2 0.8 reshape.1650
  8.8 114.7 %all_gather.12 = f32[32,4096]{1,0:T(8,128)S(1)} all-gather(f32[32,128]{1,0:T(8,128)S(1)} %get-tuple-element.319), channel_id=1, replica_groups=mesh['row'=32,'col'=16] {'row'}, dimensions={1}, use_global_device_ids=true | all-gather | bytes 540672 | tf_op jit(solution)/shard_map/all_gather | solution.py:202
  129.6 82.9 %all-gather.3.cloned.1.call-done = f32[16,32,512]{2,1,0:T(8,128)} async-done(((f32[1,32,512]{2,1,0:T(8,128)}), f32[16,32,512]{2,1,0:T(8,128)}) %all-gather.3.cloned.1.call-update) | async-done | bytes 1048592 | tf_op jit(solution)/shard_map/all_gather | solution.py:205
  212.4 1.3 reduce_sum.16
  214.5 1.1 convolution_bitcast_fusion.1
  215.5 1.1 add_select_fusion.22
  216.7 1.1 copy.300
  219.8 203.0 %reduce-scatter.3.cloned.1.call-done = f32[32,128]{1,0:T(8,128)} async-done(((f32[32,4096]{1,0:T(8,128)}), f32[32,128]{1,0:T(8,128)}) %reduce-scatter.3.cloned.1.call-update) | async-done | bytes 16400 | tf_op jit(solution)/shard_map/reduce_scatter | solution.py:210
  422.8 0.7 fusion.335
  424.1 125.7 %psum.14 = f32[2,2,32,32]{2,3,1,0:T(8,128)S(1)} all-reduce(f32[2,2,32,32]{2,3,1,0:T(8,128)S(1)} %pad_maximum_fusion.2), channel_id=1, replica_groups=mesh['row'=32,'col'=16] {'row','col'}, use_global_device_ids=true, to_apply=%region_2.4 | all-reduce | flops 4096 | bytes 32768 | tf_op jit(solution)/shard_map/psum | solution.py:212
  550.0 403.5 %while.36 = (s32[]{:T(128)}, f32[32,64]{0,1:T(8,128)S(1)}, s32[]{:T(128)}, s32[]{:T(128)}, s32[]{:T(128)}, /*index=5*/s32[]{:T(128)}, s32[]{:T(128)}, f32[]{:T(128)}, f32[]{:T(128)}, f32[]{:T(128)}, /*index=10*/f32[]{:T(128)}) while((s32[]{:T(128)}, f32[32,64]{0,1:T(8,128)S(1)}, s32[]{:T(128)}, s32[]{:T(128)}, ...), condition=%wide.region_6.8_spmd.clone.clone, body=%wide.region_3.7_spmd.clone.clone.sunk | while | flops 87498 | bytes 50118 | solution.py:83
  550.7 0.7 iota_reduce_fusion.4
  563.3 0.7 iota_reduce_fusion.4
  575.9 0.7 iota_reduce_fusion.4
  714.6 0.7 iota_reduce_fusion.4
  727.2 0.7 iota_reduce_fusion.4
  739.8 0.7 iota_reduce_fusion.4
  752.4 0.7 iota_reduce_fusion.4
  765.0 0.7 iota_reduce_fusion.4
  777.6 0.7 iota_reduce_fusion.4
  790.2 0.7 iota_reduce_fusion.4
  802.8 0.7 iota_reduce_fusion.4
  955.9 102.5 %all_gather.14 = f32[32,4096]{1,0:T(8,128)S(1)} all-gather(f32[32,128]{1,0:T(8,128)S(1)} %get-tuple-element.280), channel_id=1, replica_groups=mesh['row'=32,'col'=16] {'row'}, dimensions={1}, use_global_device_ids=true | all-gather | bytes 540672 | tf_op jit(solution)/shard_map/all_gather | solution.py:202
  1062.1 85.4 %all-gather.5.cloned.1.call-done = f32[16,32,512]{2,1,0:T(8,128)} async-done(((f32[1,32,512]{2,1,0:T(8,128)}), f32[16,32,512]{2,1,0:T(8,128)}) %all-gather.5.cloned.1.call-update) | async-done | bytes 1048592 | tf_op jit(solution)/shard_map/all_gather | solution.py:205
  1147.5 1.3 reduce_sum.20
  1149.0 1.1 convolution_bitcast_fusion
  1150.1 1.1 add_select_fusion.18
  1151.3 1.1 copy.299
  1153.7 203.7 %reduce-scatter.5.cloned.1.call-done = f32[32,128]{1,0:T(8,128)} async-done(((f32[32,4096]{1,0:T(8,128)}), f32[32,128]{1,0:T(8,128)}) %reduce-scatter.5.cloned.1.call-update) | async-done | bytes 16400 | tf_op jit(solution)/shard_map/reduce_scatter | solution.py:210
  1357.4 0.7 fusion.339
  1358.7 125.7 %psum.15 = f32[2,2,32,32]{2,3,1,0:T(8,128)S(1)} all-reduce(f32[2,2,32,32]{2,3,1,0:T(8,128)S(1)} %pad_maximum_fusion.3), channel_id=1, replica_groups=mesh['row'=32,'col'=16] {'row','col'}, use_global_device_ids=true, to_apply=%region_9.11 | all-reduce | flops 4096 | bytes 32768 | tf_op jit(solution)/shard_map/psum | solution.py:212
  1484.6 413.9 %while.37 = (s32[]{:T(128)}, f32[32,64]{0,1:T(8,128)S(1)}, s32[]{:T(128)}, s32[]{:T(128)}, s32[]{:T(128)}, /*index=5*/s32[]{:T(128)}, s32[]{:T(128)}, f32[]{:T(128)}, f32[]{:T(128)}, f32[]{:T(128)}, /*index=10*/f32[]{:T(128)}) while((s32[]{:T(128)}, f32[32,64]{0,1:T(8,128)S(1)}, s32[]{:T(128)}, s32[]{:T(128)}, ...), condition=%wide.region_13.15_spmd.clone.clone, body=%wide.region_10.14_spmd.clone.clone.sunk | while | flops 87498 | bytes 50118 | solution.py:83
  (708 shorter events, 182.8 us)
Async XLA Ops:
  7.2 116.5 %copy-start = (s32[4,4,128,128]{3,2,1,0:T(8,128)S(1)}, s32[4,4,128,128]{3,2,1,0:T(8,128)}, u32[]{:S(2)}) copy-start(s32[4,4,128,128]{3,2,1,0:T(8,128)} %param.15) | copy-start | bytes 3145732
  7.2 205.2 %all-gather.3.cloned.1.call-start = ((), (), s32[]{:S(2)}) async-start(), calls=%async_computation.2 | async-start | bytes 1114112 | tf_op jit(solution)/shard_map/all_gather | solution.py:205
  125.8 0.7 copy-start.5
  125.8 0.8 copy-start.6
  125.8 297.0 %reduce-scatter.3.cloned.1.call-start = ((), (), s32[]{:S(2)}) async-start(), calls=%async_computation.3 | async-start | bytes 540672 | tf_op jit(solution)/shard_map/reduce_scatter | solution.py:210
  126.6 0.7 copy-start.7
  127.3 0.7 copy-start.8
  213.8 0.7 copy-start.4
  217.8 929.7 %all-gather.5.cloned.1.call-start = ((), (), s32[]{:S(2)}) async-start(), calls=%async_computation.4 | async-start | bytes 1114112 | tf_op jit(solution)/shard_map/all_gather | solution.py:205
  218.4 0.7 copy-start.9
  218.4 0.7 copy-start.10
  219.1 0.7 copy-start.1
  955.1 0.7 copy-start.3
  1060.6 296.9 %reduce-scatter.5.cloned.1.call-start = ((), (), s32[]{:S(2)}) async-start(), calls=%async_computation.5 | async-start | bytes 540672 | tf_op jit(solution)/shard_map/reduce_scatter | solution.py:210
  1900.0 0.7 copy-start.2
Sparse Core Ops, SparseCore 0:
  125.9 86.4 all-gather.2
  217.9 204.8 reduce-scatter.2
  1060.7 86.7 all-gather.4
  1152.5 204.8 reduce-scatter.4
